TPU v7x, 32 devices: a whole 2x2x4 slice. The times are simulated.
32 devices in a mesh: sub: 8 (over z, y), mode: 4 (over x, core).
Axes of the slice: x: 2, y: 2, z: 4, core: 2. Of those that a mesh axis runs over, the one named last changes fastest.
Arguments:
- panels: bfloat16 [8, 2048, 768], P('sub', 'mode'), may hold values from -0.59765625 to 0.59765625
- eigvals: float32 [8, 2048], P('sub', 'mode'), may hold values from 0.5 to 20
- counts: int32 [8], P('sub'), may hold values from 512 to 2048, as said below
- separator_diag: float32 [8, 768], P('sub'), may hold values from 4 to 8
- separator_index_tables: int32 [8, 768], replicated, may hold values from 0 to 767, each once within a row
Outputs:
- condensed: float32 [768, 768], P('sub')
Inputs may be any that keep to these rules, and one draw needn't show every extreme that they name: `counts`: every value from 512 to 2048 can occur, and both ends occur in every draw. `separator_index_tables`: each row is a permutation of 0 to 767.
All inputs are finite; a program needn't handle non-finite values.
Results may differ from a plain program's by a relative error of at most 0.0003.
Values sent between devices are 32-bit elements; how exact they have to be, the bound alone decides.
A program may use at most 64 MiB of HBM per device.

v0:
```python
import math
import jax
import jax.numpy as jnp
from jax import lax
from jax.sharding import PartitionSpec as P


def from_partner(array, axis, stride):
    return lax.ppermute(array, axis, [(i, i ^ 1 << stride) for i in range(lax.axis_size(axis))])


def select_permutation(separator_index_tables, level_number, tree_node_index):
    span_rows = 2**level_number
    map_row = tree_node_index * span_rows + span_rows - 1
    base_perm = lax.dynamic_index_in_dim(separator_index_tables, map_row, 0, keepdims=False)
    sep_width = separator_index_tables.shape[1]
    shifted = (jnp.arange(sep_width, dtype=jnp.int32) + 97 * level_number % sep_width) % sep_width
    return jnp.take(base_perm, shifted)


def relabel_equations(schur_remainder_patch, arrangement_list):
    rows_first = jnp.take(schur_remainder_patch, arrangement_list, axis=0)
    return jnp.take(rows_first.T, arrangement_list, axis=0).T


def local(panels, eigvals, counts, separator_diag, separator_index_tables):
    sub_here = lax.axis_index("sub")
    mode_here = lax.axis_index("mode")
    sub_dev = panels.shape[0]
    mode_dev = panels.shape[1]
    sep_width = panels.shape[2]
    mode_start = mode_here * mode_dev
    diag_on = (mode_here == 0).astype(jnp.float32)
    contract = (((0,), (0,)), ((), ()))
    first_leaf = sub_here * sub_dev
    stack_nodes = []
    panel_rows = panels[0]
    live_count = counts[0]
    live_mask = (mode_start + jnp.arange(mode_dev, dtype=jnp.int32) < live_count).astype(
        jnp.float32
    )
    weighted = (panel_rows.astype(jnp.float32) * (live_mask / eigvals[0])[:, None]).astype(
        jnp.bfloat16
    )
    partial_sum = lax.dot_general(
        weighted, panel_rows, contract, preferred_element_type=jnp.float32
    )
    stack_nodes.append((0, diag_on * jnp.diag(separator_diag[0]) - partial_sum))
    while len(stack_nodes) >= 2 and stack_nodes[-1][0] == stack_nodes[-2][0]:
        level_number, right_matrix_tile = stack_nodes.pop()
        level_same, left_matrix_tile = stack_nodes.pop()
        span_leaves = 2 ** (level_number + 1)
        left_child_node = first_leaf // 2**level_number + 2 * ((1 - span_leaves) // span_leaves)
        reordered_first_factor = relabel_equations(
            left_matrix_tile,
            select_permutation(separator_index_tables, level_number, left_child_node),
        )
        reordered_second_factor = relabel_equations(
            right_matrix_tile,
            select_permutation(separator_index_tables, level_number, left_child_node + 1),
        )
        stack_nodes.append((level_number + 1, reordered_first_factor + reordered_second_factor))
    device_level_count, schur_remainder_patch = stack_nodes[0]
    sub_count = lax.axis_size("sub")
    sub_bits = sub_count.bit_length() - 1
    schur_remainder_patch = lax.psum(schur_remainder_patch, "mode")
    for bit_position in range(sub_bits):
        tree_node_index = sub_here // 2**bit_position
        schur_remainder_patch = relabel_equations(
            schur_remainder_patch,
            select_permutation(
                separator_index_tables, device_level_count + bit_position, tree_node_index
            ),
        )
        schur_remainder_patch = schur_remainder_patch + from_partner(
            schur_remainder_patch, "sub", bit_position
        )
    own_rows = sep_width // sub_count
    own_block = lax.dynamic_slice_in_dim(schur_remainder_patch, sub_here * own_rows, own_rows, 0)
    return own_block * (1.0 / math.sqrt(sub_dev * sub_count))


def solution(mesh):
    return jax.shard_map(
        local,
        mesh=mesh,
        in_specs=(P("sub", "mode", None), P("sub", "mode"), P("sub"), P("sub", None), P()),
        out_specs=P("sub", None),
        check_vma=False,
    )
```

profile of v0, /device:TPU:0, one launch (start us, length us, event | category | flops | bytes accessed | tf_op | source)
XLA Modules:
  0.0 345.9 jit_solution(12305404054721332280)
XLA Ops:
  6.5 0.0 all-reduce.2.cloned.1.call-start
  7.2 0.7 reduce.3
  7.9 0.7 convert_divide_fusion
  8.6 3.7 %multiply_subtract_fusion = f32[768,768]{1,0:T(8,128)} fusion(f32[768]{0:T(1024)S(1)} %reduce.3, f32[]{:T(128)S(6)} %convert_element_type.20, bf16[1,512,768]{2,1,0:T(8,128)(2,1)} %param.9, f32[512]{0:T(512)S(1)} %convert_divide_fusion), kind=kOutput, calls=%fused_computation.15 | convolution fusion | flops 607518720 | bytes 3150852 | tf_op jit(solution)/shard_map/dot_general | solution.py:45
  12.3 0.0 all-reduce.2.cloned.1.call-update
  12.4 0.9 dynamic-slice_reduce_fusion
  13.3 3.2 gather_fusion
  16.5 54.3 %all-reduce.2.cloned.1.call-done = f32[768,768]{1,0:T(8,128)} async-done(((f32[768,768]{1,0:T(8,128)}), f32[768,768]{1,0:T(8,128)}) %all-reduce.2.cloned.1.call-update) | async-done | bytes 2359312 | tf_op jit(solution)/shard_map/psum | solution.py:66
  70.8 5.1 %gather_fusion.1 = f32[768,768]{1,0:T(8,128)S(1)} fusion(f32[768,768]{1,0:T(8,128)} %all-reduce.2.cloned.1.call-done, s32[1024]{0:T(1024)S(1)} %pad_clamp_fusion.2), kind=kCustom, calls=%fused_computation.1.clone | custom fusion | bytes 4721664 | tf_op jit(solution)/shard_map/jit(_take)/gather | solution.py:22
  76.0 1.6 select_bitcast_fusion.5
  77.6 2.0 copy.18
  79.7 3.5 %gather_fusion.2 = f32[768,768]{1,0:T(8,128)} fusion(f32[768,768]{1,0:T(8,128)S(1)} %copy.18, s32[1024]{0:T(1024)S(1)} %pad_clamp_fusion.2), kind=kCustom, calls=%fused_computation.4.clone | custom fusion | bytes 4721664 | tf_op jit(solution)/shard_map/jit(_take)/gather | solution.py:23
  83.1 3.3 select_bitcast_fusion.4
  86.5 0.0 copy-start.1
  86.5 1.5 collective-permute-start
  88.0 3.2 gather_fusion.3
  91.2 48.5 %collective-permute-done = f32[768,768]{0,1:T(8,128)} collective-permute-done((f32[768,768]{0,1:T(8,128)}, f32[768,768]{0,1:T(8,128)}, u32[]{:S(2)}, u32[]{:S(2)}) %collective-permute-start) | collective-permute-done | bytes 2359328 | tf_op jit(solution)/shard_map/ppermute | solution.py:9
  139.7 0.0 copy-done.1
  139.7 3.5 %fusion.12 = f32[768,768]{0,1:T(8,128)} fusion(f32[768,768]{0,1:T(8,128)} %collective-permute-done, f32[768,768]{1,0:T(8,128)S(1)} %copy-done.1, pred[768]{0:T(1024)(128)(4,1)S(1)} %compare_and_fusion.2), kind=kLoop, calls=%fused_computation.53 | loop fusion | flops 1179648 | bytes 7078656 | tf_op jit(solution)/shard_map/add | solution.py:75
  143.2 2.0 copy.19
  145.2 3.5 %gather_fusion.4 = f32[768,768]{1,0:T(8,128)} fusion(f32[768,768]{1,0:T(8,128)S(1)} %copy.19, s32[1024]{0:T(1024)S(1)} %pad_clamp_fusion.1), kind=kCustom, calls=%fused_computation.5.clone | custom fusion | bytes 4721664 | tf_op jit(solution)/shard_map/jit(_take)/gather | solution.py:22
  148.7 3.3 select_bitcast_fusion.3
  152.0 2.0 copy.20
  154.0 3.5 %gather_fusion.5 = f32[768,768]{1,0:T(8,128)} fusion(f32[768,768]{1,0:T(8,128)S(1)} %copy.20, s32[1024]{0:T(1024)S(1)} %pad_clamp_fusion.1), kind=kCustom, calls=%fused_computation.6.clone | custom fusion | bytes 4721664 | tf_op jit(solution)/shard_map/jit(_take)/gather | solution.py:23
  157.5 3.3 select_bitcast_fusion.2
  160.8 0.0 copy-start
  160.8 1.5 collective-permute-start.1
  162.3 3.2 gather_fusion.6
  165.6 47.6 %collective-permute-done.1 = f32[768,768]{0,1:T(8,128)} collective-permute-done((f32[768,768]{0,1:T(8,128)}, f32[768,768]{0,1:T(8,128)}, u32[]{:S(2)}, u32[]{:S(2)}) %collective-permute-start.1) | collective-permute-done | bytes 2359328 | tf_op jit(solution)/shard_map/ppermute | solution.py:9
  213.2 0.0 copy-done
  213.2 3.4 fusion.11
  216.6 2.0 copy.21
  218.6 3.5 %gather_fusion.7 = f32[768,768]{1,0:T(8,128)} fusion(f32[768,768]{1,0:T(8,128)S(1)} %copy.21, s32[1024]{0:T(1024)S(1)} %pad_clamp_fusion), kind=kCustom, calls=%fused_computation.7.clone | custom fusion | bytes 4721664 | tf_op jit(solution)/shard_map/jit(_take)/gather | solution.py:22
  222.1 3.3 select_bitcast_fusion.1
  225.4 2.0 copy.22
  227.5 3.5 %gather_fusion.8 = f32[768,768]{1,0:T(8,128)} fusion(f32[768,768]{1,0:T(8,128)S(1)} %copy.22, s32[1024]{0:T(1024)S(1)} %pad_clamp_fusion), kind=kCustom, calls=%fused_computation.8.clone | custom fusion | bytes 4721664 | tf_op jit(solution)/shard_map/jit(_take)/gather | solution.py:23
  230.9 2.0 copy.23
  233.0 1.6 select_bitcast_fusion
  234.5 2.4 collective-permute-start.2
  236.9 100.4 %collective-permute-done.2 = f32[768,768]{1,0:T(8,128)S(1)} collective-permute-done((f32[768,768]{1,0:T(8,128)}, f32[768,768]{1,0:T(8,128)S(1)}, u32[]{:S(2)}, u32[]{:S(2)}) %collective-permute-start.2) | collective-permute-done | bytes 2359328 | tf_op jit(solution)/shard_map/ppermute | solution.py:9
  337.3 1.7 fusion.4
  (15 shorter events, 0.1 us)
Async XLA Ops:
  6.5 64.3 %all-reduce.2.cloned.1.call-start = ((), (), s32[]{:S(2)}) async-start(), calls=%async_computation | async-start | bytes 4718592 | tf_op jit(solution)/shard_map/psum | solution.py:66
  86.5 53.2 %copy-start.1 = (f32[768,768]{1,0:T(8,128)S(1)}, f32[768,768]{1,0:T(8,128)}, u32[]{:S(2)}) copy-start(f32[768,768]{1,0:T(8,128)} %gather_fusion.2) | copy-start | bytes 7077892
  86.5 53.2 %collective-permute-start = (f32[768,768]{0,1:T(8,128)}, f32[768,768]{0,1:T(8,128)}, u32[]{:S(2)}, u32[]{:S(2)}) collective-permute-start(f32[768,768]{0,1:T(8,128)} %select_bitcast_fusion.4), channel_id=1, source_target_pairs={{0,4},{4,0},{8,12},{12,8},{16,20},{20,16},{24,28},{28,24},{1,5},{5... | collective-permute-start | bytes 7077896 | tf_op jit(solution)/shard_map/ppermute | solution.py:9
  160.8 52.3 %copy-start = (f32[768,768]{1,0:T(8,128)S(1)}, f32[768,768]{1,0:T(8,128)}, u32[]{:S(2)}) copy-start(f32[768,768]{1,0:T(8,128)} %gather_fusion.5) | copy-start | bytes 7077892
  160.8 52.3 %collective-permute-start.1 = (f32[768,768]{0,1:T(8,128)}, f32[768,768]{0,1:T(8,128)}, u32[]{:S(2)}, u32[]{:S(2)}) collective-permute-start(f32[768,768]{0,1:T(8,128)} %select_bitcast_fusion.2), channel_id=1, source_target_pairs={{0,8},{4,12},{8,0},{12,4},{16,24},{20,28},{24,16},{28,20},{1,9},{5... | collective-permute-start | bytes 7077896 | tf_op jit(solution)/shard_map/ppermute | solution.py:9
  234.5 102.8 %collective-permute-start.2 = (f32[768,768]{1,0:T(8,128)}, f32[768,768]{1,0:T(8,128)S(1)}, u32[]{:S(2)}, u32[]{:S(2)}) collective-permute-start(f32[768,768]{1,0:T(8,128)} %select_bitcast_fusion), channel_id=1, source_target_pairs={{0,16},{4,20},{8,24},{12,28},{16,0},{20,4},{24,8},{28,12},{1,17},{... | collective-permute-start | bytes 7077896 | tf_op jit(solution)/shard_map/ppermute | solution.py:9
Sparse Core Ops, SparseCore 0:
  12.5 58.3 all-reduce.1
where the time goes:
time: 347 us; the launch traced here: 346 us
  waiting for transfers between devices  251 us (72%)
  local copies, waits for them, and re-layouts  45.1 us (13%)
  other arithmetic  26.7 us (8%)
  between operations  14.2 us (4%)
  starting transfers between devices  5.37 us (2%)
  matrix products  3.73 us (1%)
    ppermute x3, waiting for transfers between devices, from_partner(): lax.ppermute(array, axis, [(i, i ^ 1 << stride) for i in range(lax.axis_s...  196 us
    psum x1, waiting for transfers between devices, local(): schur_remainder_patch = lax.psum(schur_remainder_patch, 'mode')  54.3 us
    transpose x6, other arithmetic, relabel_equations(): return jnp.take(rows_first.T, arrangement_list, axis=0).T  16.5 us
    gather x4, local copies, waits for them, and re-layouts, relabel_equations(): return jnp.take(rows_first.T, arrangement_list, axis=0).T  12.4 us
    gather x3, local copies, waits for them, and re-layouts, relabel_equations(): rows_first = jnp.take(schur_remainder_patch, arrangement_list, axis=0)  12.1 us
    gather x3, local copies, waits for them, and re-layouts, select_permutation(): return jnp.take(base_perm, shifted)  9.56 us
  transfers between devices with their start and end apart: 4, of which 4 were waited for; matrix products, arithmetic and copies ran while one was open for 3% of the time, Pallas kernels for 0%

commit v1 on v0

--- a/solution.py
+++ b/solution.py
@@ -63,7 +63,7 @@
     device_level_count, schur_remainder_patch = stack_nodes[0]
     sub_count = lax.axis_size("sub")
     sub_bits = sub_count.bit_length() - 1
-    schur_remainder_patch = lax.psum(schur_remainder_patch, "mode")
+    schur_remainder_patch = jnp.sum(jax.lax.all_gather(schur_remainder_patch, axis_name="mode"), 0)
     for bit_position in range(sub_bits):
         tree_node_index = sub_here // 2**bit_position
         schur_remainder_patch = relabel_equations(

time: 347 us -> 362 us (1.043)
  waiting for transfers between devices: 251 us -> 261 us
  other arithmetic: 26.7 us -> 33 us
    all_gather x0 -> x1, waiting for transfers between devices: none -> 62.9 us  [local(): jax.lax.all_gather(schur_remainder_patch, axis_name='mode')]
    psum x1 -> x0, waiting for transfers between devices: 54.3 us -> none  [local(): schur_remainder_patch = lax.psum(schur_remainder_patch, 'mode')]
    reduce_sum x0 -> x1, other arithmetic: none -> 4.7 us  [local(): jnp.sum(jax.lax.all_gather(schur_remainder_patch, axis_name='mode'), 0)]
where the time goes in v1:
time: 362 us; the launch traced here: 361 us
  waiting for transfers between devices  261 us (72%)
  local copies, waits for them, and re-layouts  43.4 us (12%)
  other arithmetic  33 us (9%)
  between operations  14.2 us (4%)
  starting transfers between devices  5.37 us (1%)
  matrix products  3.72 us (1%)
    ppermute x3, waiting for transfers between devices, from_partner(): lax.ppermute(array, axis, [(i, i ^ 1 << stride) for i in range(lax.axis_s...  198 us
    all_gather x1, waiting for transfers between devices, local(): jax.lax.all_gather(schur_remainder_patch, axis_name='mode')  62.9 us
    transpose x6, other arithmetic, relabel_equations(): return jnp.take(rows_first.T, arrangement_list, axis=0).T  18.2 us
    gather x4, local copies, waits for them, and re-layouts, relabel_equations(): return jnp.take(rows_first.T, arrangement_list, axis=0).T  12.4 us
    gather x3, local copies, waits for them, and re-layouts, relabel_equations(): rows_first = jnp.take(schur_remainder_patch, arrangement_list, axis=0)  10.4 us
    gather x3, local copies, waits for them, and re-layouts, select_permutation(): return jnp.take(base_perm, shifted)  9.56 us
  transfers between devices with their start and end apart: 4, of which 4 were waited for; matrix products, arithmetic and copies ran while one was open for 3% of the time, Pallas kernels for 0%

profile of v1, /device:TPU:0, one launch (start us, length us, event | category | flops | bytes accessed | tf_op | source)
XLA Modules:
  0.0 360.8 jit_solution(11531159904679365215)
XLA Ops:
  6.5 0.0 all-gather.3.cloned.1.call-start
  7.2 0.7 reduce.3
  7.9 0.7 convert_divide_fusion
  8.6 3.7 %multiply_subtract_fusion = f32[768,768]{1,0:T(8,128)} fusion(f32[768]{0:T(1024)S(1)} %reduce.3, f32[]{:T(128)S(6)} %convert_element_type.20, bf16[1,512,768]{2,1,0:T(8,128)(2,1)} %param.9, f32[512]{0:T(512)S(1)} %convert_divide_fusion), kind=kOutput, calls=%fused_computation.15 | convolution fusion | flops 607518720 | bytes 3150852 | tf_op jit(solution)/shard_map/dot_general | solution.py:45
  12.3 0.0 all-gather.3.cloned.1.call-update
  12.4 0.9 dynamic-slice_reduce_fusion
  13.3 3.2 gather_fusion
  16.5 62.9 %all-gather.3.cloned.1.call-done = f32[3072,768]{1,0:T(8,128)} async-done(((f32[768,768]{1,0:T(8,128)}), f32[3072,768]{1,0:T(8,128)}) %all-gather.3.cloned.1.call-update) | async-done | bytes 9437200 | tf_op jit(solution)/shard_map/all_gather | solution.py:66
  79.4 4.7 %reduce_sum.9 = f32[768,768]{1,0:T(8,128)S(1)} reduce(f32[4,768,768]{2,1,0:T(8,128)} %bitcast.26, f32[]{:T(128)} %constant.99.clone.1), dimensions={0}, to_apply=%region_0.1 | reduce | flops 1769472 | bytes 11796484 | tf_op jit(solution)/shard_map/reduce_sum | solution.py:66
  84.1 3.5 gather_fusion.1
  87.6 3.3 select_bitcast_fusion.5
  90.9 2.0 copy.18
  92.9 3.5 gather_fusion.2
  96.4 3.3 select_bitcast_fusion.4
  99.7 0.0 copy-start.1
  99.7 1.5 collective-permute-start
  101.2 3.2 gather_fusion.3
  104.5 49.0 %collective-permute-done = f32[768,768]{0,1:T(8,128)} collective-permute-done((f32[768,768]{0,1:T(8,128)}, f32[768,768]{0,1:T(8,128)}, u32[]{:S(2)}, u32[]{:S(2)}) %collective-permute-start) | collective-permute-done | bytes 2359328 | tf_op jit(solution)/shard_map/ppermute | solution.py:9
  153.5 0.0 copy-done.1
  153.5 3.5 fusion.12
  157.0 2.0 copy.19
  159.0 3.5 gather_fusion.4
  162.5 3.3 select_bitcast_fusion.3
  165.8 2.0 copy.20
  167.8 3.5 gather_fusion.5
  171.3 3.3 select_bitcast_fusion.2
  174.6 0.0 copy-start
  174.6 1.5 collective-permute-start.1
  176.1 3.2 gather_fusion.6
  179.4 48.2 %collective-permute-done.1 = f32[768,768]{0,1:T(8,128)} collective-permute-done((f32[768,768]{0,1:T(8,128)}, f32[768,768]{0,1:T(8,128)}, u32[]{:S(2)}, u32[]{:S(2)}) %collective-permute-start.1) | collective-permute-done | bytes 2359328 | tf_op jit(solution)/shard_map/ppermute | solution.py:9
  227.5 0.0 copy-done
  227.5 3.4 fusion.11
  231.0 2.0 copy.21
  233.0 3.5 gather_fusion.7
  236.5 3.3 select_bitcast_fusion.1
  239.8 2.0 copy.22
  241.8 3.5 gather_fusion.8
  245.3 2.0 copy.23
  247.3 1.6 select_bitcast_fusion
  248.9 2.4 collective-permute-start.2
  251.3 100.9 %collective-permute-done.2 = f32[768,768]{1,0:T(8,128)S(1)} collective-permute-done((f32[768,768]{1,0:T(8,128)}, f32[768,768]{1,0:T(8,128)S(1)}, u32[]{:S(2)}, u32[]{:S(2)}) %collective-permute-start.2) | collective-permute-done | bytes 2359328 | tf_op jit(solution)/shard_map/ppermute | solution.py:9
  352.2 1.7 fusion.4
  (15 shorter events, 0.1 us)
Async XLA Ops:
  6.5 72.9 %all-gather.3.cloned.1.call-start = ((), (), s32[]{:S(2)}) async-start(), calls=%async_computation | async-start | bytes 11796480 | tf_op jit(solution)/shard_map/all_gather | solution.py:66
  99.7 53.7 %copy-start.1 = (f32[768,768]{1,0:T(8,128)S(1)}, f32[768,768]{1,0:T(8,128)}, u32[]{:S(2)}) copy-start(f32[768,768]{1,0:T(8,128)} %gather_fusion.2) | copy-start | bytes 7077892
  99.7 53.7 %collective-permute-start = (f32[768,768]{0,1:T(8,128)}, f32[768,768]{0,1:T(8,128)}, u32[]{:S(2)}, u32[]{:S(2)}) collective-permute-start(f32[768,768]{0,1:T(8,128)} %select_bitcast_fusion.4), channel_id=1, source_target_pairs={{0,4},{4,0},{8,12},{12,8},{16,20},{20,16},{24,28},{28,24},{1,5},{5... | collective-permute-start | bytes 7077896 | tf_op jit(solution)/shard_map/ppermute | solution.py:9
  174.6 52.9 %copy-start = (f32[768,768]{1,0:T(8,128)S(1)}, f32[768,768]{1,0:T(8,128)}, u32[]{:S(2)}) copy-start(f32[768,768]{1,0:T(8,128)} %gather_fusion.5) | copy-start | bytes 7077892
  174.6 52.9 %collective-permute-start.1 = (f32[768,768]{0,1:T(8,128)}, f32[768,768]{0,1:T(8,128)}, u32[]{:S(2)}, u32[]{:S(2)}) collective-permute-start(f32[768,768]{0,1:T(8,128)} %select_bitcast_fusion.2), channel_id=1, source_target_pairs={{0,8},{4,12},{8,0},{12,4},{16,24},{20,28},{24,16},{28,20},{1,9},{5... | collective-permute-start | bytes 7077896 | tf_op jit(solution)/shard_map/ppermute | solution.py:9
  248.9 103.3 %collective-permute-start.2 = (f32[768,768]{1,0:T(8,128)}, f32[768,768]{1,0:T(8,128)S(1)}, u32[]{:S(2)}, u32[]{:S(2)}) collective-permute-start(f32[768,768]{1,0:T(8,128)} %select_bitcast_fusion), channel_id=1, source_target_pairs={{0,16},{4,20},{8,24},{12,28},{16,0},{20,4},{24,8},{28,12},{1,17},{... | collective-permute-start | bytes 7077896 | tf_op jit(solution)/shard_map/ppermute | solution.py:9
Sparse Core Ops, SparseCore 0:
  12.4 66.9 all-gather.2
